TPU v7x, 32 devices: a whole 2x2x4 slice. The times are simulated.
32 devices in a mesh: groups: 2 (over y), dp: 4 (over x, core), tensor: 4 (over z).
Axes of the slice: x: 2, y: 2, z: 4, core: 2. Of those that a mesh axis runs over, the one named last changes fastest.
Arguments:
- inputs: bfloat16 [4096, 4096], P(('groups', 'dp'), 'tensor'), parts along dimension 0, may hold values from -6 to 6
- out_grads: bfloat16 [4096, 4096], P(('groups', 'dp'), 'tensor'), parts along dimension 0, may hold values from -6 to 6
- example_ids: int32 [8, 512], P(('groups', 'dp')), parts along dimension 0, may hold values from 0 to 15, never falling along the last dimension, each value on 1 to 64 neighbouring positions
- query_inputs: bfloat16 [2048, 4096], P(('groups', 'dp'), 'tensor'), parts along dimension 0, may hold values from -6 to 6
- query_grads: bfloat16 [2048, 4096], P(('groups', 'dp'), 'tensor'), parts along dimension 0, may hold values from -6 to 6
- query_ids: int32 [8, 256], P(('groups', 'dp')), parts along dimension 0, may hold values from 0 to 15, never falling along the last dimension, each value on 1 to 32 neighbouring positions
- w_gate: bfloat16 [4096, 14336], P('dp', 'tensor'), may hold values from -0.09375 to 0.09375
- w_up: bfloat16 [4096, 14336], P('dp', 'tensor'), may hold values from -0.09375 to 0.09375
- in_project: bfloat16 [64, 14336], P(None, 'tensor'), may hold values from -0.046875 to 0.046875
- out_project: bfloat16 [64, 4096], P(None, 'tensor'), may hold values from -0.09375 to 0.09375
Outputs:
- sketches: float32 [128, 4096], P(('groups', 'dp')), parts along dimension 0
- scores: float32 [128, 64], P(('groups', 'dp')), parts along dimension 0
There are 2 independent parts, one for each index of `groups`. A program takes and returns all parts, laid end to end along the dimension named above; an argument that names none is the same for every part. Nothing has to cross between parts.
Inputs may be any that keep to these rules, and one draw needn't show every extreme that they name: `example_ids`: row k holds the tokens of index k of dp: 16 training examples of consecutive tokens, numbered in order from 0, each of 1 to 64 tokens. `query_ids`: row k holds the tokens of index k of dp: 16 queries of consecutive tokens, numbered in order from 0, each of 1 to 32 tokens.
All inputs are finite; a program needn't handle non-finite values.
Results may differ from a plain program's by a relative error of at most 0.004.
Values may be sent and summed in bfloat16 or wider, within the bound.
A program may use at most 192 MiB of HBM per device.

v0:
```python
import jax
import jax.numpy as jnp
from jax import lax
from jax.sharding import PartitionSpec as P

EX_DEV = 16
QEX_DEV = 16


def sketch_from(left, right, onehot):
    count = onehot.shape[1]
    spread = (onehot[:, :, None] * left[:, None, :]).reshape(left.shape[0], count * left.shape[1])
    return jnp.dot(spread.T, right, precision=lax.Precision.HIGHEST).reshape(
        count, left.shape[1] * right.shape[1]
    )


def member_table(ids, count):
    return (ids[:, None] == jnp.arange(count, dtype=jnp.int32)[None, :]).astype(jnp.float32)


def local(
    inputs,
    out_grads,
    example_ids,
    query_inputs,
    query_grads,
    query_ids,
    w_gate,
    w_up,
    in_project,
    out_project,
):
    full_train, full_query = (
        lax.all_gather(inputs, "tensor", axis=1, tiled=True),
        lax.all_gather(query_inputs, "tensor", axis=1, tiled=True),
    )
    all_tokens = jnp.concatenate([full_train, full_query], 0)
    gate_act = jnp.dot(
        all_tokens,
        lax.all_gather(w_gate, "dp", axis=0, tiled=True),
        preferred_element_type=jnp.float32,
    )
    up_act = jnp.dot(
        all_tokens,
        lax.all_gather(w_up, "dp", axis=0, tiled=True),
        preferred_element_type=jnp.float32,
    )
    hidden = (jax.nn.silu(gate_act) * up_act).astype(jnp.bfloat16)
    all_grads = jnp.concatenate([out_grads, query_grads], 0)
    partial_sum = jnp.concatenate(
        [
            jnp.dot(all_grads, out_project.T, preferred_element_type=jnp.float32),
            jnp.dot(hidden, in_project.T, preferred_element_type=jnp.float32),
        ],
        1,
    )
    projected = lax.psum(partial_sum, "tensor")
    rank = in_project.shape[0]
    train_rows = inputs.shape[0]
    sketches = sketch_from(
        projected[:train_rows, :rank],
        projected[:train_rows, rank:],
        member_table(example_ids[0], EX_DEV),
    )
    query_part = projected[train_rows:]
    query_table = member_table(query_ids[0], QEX_DEV)
    local_sketch = sketch_from(query_part[:, :rank], query_part[:, rank:], query_table)
    query_sketches = lax.all_gather(local_sketch, "dp", axis=0, tiled=True)
    train_norm = jnp.sqrt(jnp.sum(sketches * sketches, axis=1) + 1e-06)
    query_norm = jnp.sqrt(jnp.sum(query_sketches * query_sketches, axis=1) + 1e-06)
    inner = jnp.dot(sketches, query_sketches.T, precision=lax.Precision.HIGHEST)
    scores = rank * inner / (train_norm[:, None] * query_norm[None, :])
    return (sketches, scores)


def solution(mesh):
    in_specs = (
        P(("groups", "dp"), "tensor"),
        P(("groups", "dp"), "tensor"),
        P(("groups", "dp"), None),
        P(("groups", "dp"), "tensor"),
        P(("groups", "dp"), "tensor"),
        P(("groups", "dp"), None),
        P("dp", "tensor"),
        P("dp", "tensor"),
        P(None, "tensor"),
        P(None, "tensor"),
    )
    out_specs = (P(("groups", "dp"), None), P(("groups", "dp"), None))
    return jax.shard_map(local, mesh=mesh, in_specs=in_specs, out_specs=out_specs, check_vma=False)
```

profile of v0, /device:TPU:0, one launch (start us, length us, event | category | flops | bytes accessed | tf_op | source)
XLA Modules:
  0.0 601.4 jit_solution(18174166851194281527)
XLA Ops:
  7.2 0.7 all-gather.6.cloned.1.call-update
  8.0 0.7 all-gather.8.cloned.1.call-update
  8.7 0.7 all-gather.10.cloned.1.call-update
  9.5 0.5 all-gather.12.cloned.1.call-update
  10.1 0.6 fusion.1
  10.7 82.4 %all-gather.6.cloned.1.call-done = bf16[512,4096]{1,0:T(8,128)(2,1)} async-done(((bf16[512,1024]{1,0:T(8,128)(2,1)}), bf16[512,4096]{1,0:T(8,128)(2,1)}) %all-gather.6.cloned.1.call-update) | async-done | bytes 4194320 | tf_op jit(solution)/shard_map/all_gather | solution.py:35
  93.1 4.8 constant_dynamic-update-slice_fusion.1
  97.8 41.3 %all-gather.8.cloned.1.call-done = bf16[256,4096]{1,0:T(8,128)(2,1)} async-done(((bf16[256,1024]{1,0:T(8,128)(2,1)}), bf16[256,4096]{1,0:T(8,128)(2,1)}) %all-gather.8.cloned.1.call-update) | async-done | bytes 2097168 | tf_op jit(solution)/shard_map/all_gather | solution.py:36
  139.2 3.2 constant_dynamic-update-slice_fusion
  142.3 175.2 %all-gather.10.cloned.1.call-done = bf16[4096,3584]{1,0:T(8,128)(2,1)} async-done(((bf16[1024,3584]{1,0:T(8,128)(2,1)}), bf16[4096,3584]{1,0:T(8,128)(2,1)}) %all-gather.10.cloned.1.call-update) | async-done | bytes 29360144 | tf_op jit(solution)/shard_map/all_gather | solution.py:41
  317.5 30.1 %fusion.14 = f32[768,3584]{1,0:T(8,128)} fusion(bf16[768,4096]{1,0:T(8,128)(2,1)} %constant_dynamic-update-slice_fusion, bf16[4096,3584]{1,0:T(8,128)(2,1)} %all-gather.10.cloned.1.call-done), kind=kOutput, calls=%fused_computation.27 | convolution fusion | flops 22548578304 | bytes 46661632 | tf_op jit(solution)/shard_map/dot_general | solution.py:39
  347.6 149.3 %all-gather.12.cloned.1.call-done = bf16[4096,3584]{1,0:T(8,128)(2,1)} async-done(((bf16[1024,3584]{1,0:T(8,128)(2,1)}), bf16[4096,3584]{1,0:T(8,128)(2,1)}) %all-gather.12.cloned.1.call-update) | async-done | bytes 29360144 | tf_op jit(solution)/shard_map/all_gather | solution.py:46
  497.0 35.1 %fusion = f32[768,64]{0,1:T(8,128)S(1)} fusion(bf16[64,3584]{1,0:T(8,128)(2,1)S(1)} %copy-done, f32[768,3584]{1,0:T(8,128)} %fusion.14, bf16[768,4096]{1,0:T(8,128)(2,1)} %constant_dynamic-update-slice_fusion, bf16[4096,3584]{1,0:T(8,128)(2,1)} %all-gather.12.cloned.1.call-done), kind=kOutput, calls=%fused_computation.1 | convolution fusion | flops 22917414912 | bytes 47316992 | tf_op jit(solution)/shard_map/dot_general | solution.py:54
  532.1 0.8 pad_maximum_fusion
  533.1 37.0 %all-reduce.2.cloned.1.call-done = f32[768,128]{0,1:T(8,128)} async-done(((f32[768,128]{0,1:T(8,128)}), f32[768,128]{0,1:T(8,128)}) %all-reduce.2.cloned.1.call-update) | async-done | bytes 393232 | tf_op jit(solution)/shard_map/psum | solution.py:58
  570.1 0.9 slice.21
  571.1 1.8 fusion.8
  573.0 0.9 reshape.80
  573.9 0.9 slice.19
  574.8 0.3 broadcast_multiply_fusion
  575.1 3.1 multiply_reduce_fusion.1
  578.7 11.6 %all-gather.14.cloned.1.call-done = f32[64,4096]{1,0:T(8,128)} async-done(((f32[16,4096]{1,0:T(8,128)}), f32[64,4096]{1,0:T(8,128)}) %all-gather.14.cloned.1.call-update) | async-done | bytes 1048592 | tf_op jit(solution)/shard_map/all_gather | solution.py:69
  590.3 1.4 multiply_reduce_fusion
  591.8 2.8 fusion.5
  (33 shorter events, 1.2 us)
Async XLA Ops:
  7.2 489.8 %copy-start = (bf16[64,3584]{1,0:T(8,128)(2,1)S(1)}, bf16[64,3584]{1,0:T(8,128)(2,1)}, u32[]{:S(2)}) copy-start(bf16[64,3584]{1,0:T(8,128)(2,1)} %param.18) | copy-start | bytes 1376260
  7.2 85.9 %all-gather.6.cloned.1.call-start = ((), (), s32[]{:S(2)}) async-start(), calls=%async_computation | async-start | bytes 5242880 | tf_op jit(solution)/shard_map/all_gather | solution.py:35
  7.9 131.2 %all-gather.8.cloned.1.call-start = ((), (), s32[]{:S(2)}) async-start(), calls=%async_computation.1 | async-start | bytes 2621440 | tf_op jit(solution)/shard_map/all_gather | solution.py:36
  8.7 1.4 copy-start.5
  8.7 1.4 copy-start.6
  8.7 1.4 copy-start.7
  8.7 308.8 %all-gather.10.cloned.1.call-start = ((), (), s32[]{:S(2)}) async-start(), calls=%async_computation.2 | async-start | bytes 36700160 | tf_op jit(solution)/shard_map/all_gather | solution.py:41
  9.4 487.5 %all-gather.12.cloned.1.call-start = ((), (), s32[]{:S(2)}) async-start(), calls=%async_computation.3 | async-start | bytes 36700160 | tf_op jit(solution)/shard_map/all_gather | solution.py:46
  10.0 560.1 %all-reduce.2.cloned.1.call-start = ((), (), s32[]{:S(2)}) async-start(), calls=%async_computation.4 | async-start | bytes 786432 | tf_op jit(solution)/shard_map/psum | solution.py:58
  347.6 185.5 %copy-start.4 = (s32[1,256]{1,0:T(1,128)S(1)}, s32[1,256]{1,0:T(1,128)}, u32[]{:S(2)}) copy-start(s32[1,256]{1,0:T(1,128)} %param.15) | copy-start | bytes 3076
  347.6 226.2 %copy-start.3 = (s32[1,512]{1,0:T(1,128)S(1)}, s32[1,512]{1,0:T(1,128)}, u32[]{:S(2)}) copy-start(s32[1,512]{1,0:T(1,128)} %param.12) | copy-start | bytes 6148
  532.9 57.4 %all-gather.14.cloned.1.call-start = ((), (), s32[]{:S(2)}) async-start(), calls=%async_computation.5 | async-start | bytes 1310720 | tf_op jit(solution)/shard_map/all_gather | solution.py:69
  570.1 24.4 %copy-start.1 = (bf16[64,3584]{1,0:T(8,128)(2,1)S(1)}, bf16[64,3584]{1,0:T(8,128)(2,1)}, u32[]{:S(2)}) copy-start(bf16[64,3584]{1,0:T(8,128)(2,1)} %param.18) | copy-start | bytes 1376260
  578.5 16.0 %copy-start.2 = (f32[16,4096]{1,0:T(8,128)}, f32[16,4096]{1,0:T(8,128)S(1)}, u32[]{:S(2)}) copy-start(f32[16,4096]{1,0:T(8,128)S(1)} %reshape.79) | copy-start | bytes 786436
Sparse Core Ops, SparseCore 0:
  9.6 83.4 all-gather.5
  94.7 44.4 all-gather.7
  140.7 176.7 all-gather.9
  318.9 178.0 all-gather.11
  533.0 37.0 all-reduce.1
  574.0 16.3 all-gather.13
where the time goes:
time: 602 us; the launch traced here: 601 us
  waiting for transfers between devices  499 us (83%)
  matrix products  73.5 us (12%)
  between operations  14.3 us (2%)
  local copies, waits for them, and re-layouts  11.1 us (2%)
    all_gather x1, waiting for transfers between devices, local(): lax.all_gather(w_gate, 'dp', axis=0, tiled=True)  175 us
    all_gather x1, waiting for transfers between devices, local(): lax.all_gather(w_up, 'dp', axis=0, tiled=True)  149 us
    all_gather x1, waiting for transfers between devices, local(): lax.all_gather(inputs, 'tensor', axis=1, tiled=True)  82.4 us
    all_gather x1, waiting for transfers between devices, local(): lax.all_gather(query_inputs, 'tensor', axis=1, tiled=True)  41.3 us
    psum x1, waiting for transfers between devices, local(): projected = lax.psum(partial_sum, 'tensor')  37 us
    dot_general x1, matrix products, local(): jnp.dot(hidden, in_project.T, preferred_element_type=jnp.float32)  35.1 us
    dot_general x1, matrix products, local(): jnp.dot(all_tokens, lax.all_gather(w_gate, 'dp', axis=0, tiled=True), pre...  30.1 us
  transfers between devices with their start and end apart: 6, of which 6 were waited for; matrix products, arithmetic and copies ran while one was open for 7% of the time, Pallas kernels for 0%

commit v1 on v0

--- a/solution.py
+++ b/solution.py
@@ -1,6 +1,10 @@
+import functools
+
 import jax
 import jax.numpy as jnp
 from jax import lax
+from jax.experimental import pallas as pl
+from jax.experimental.pallas import tpu as pltpu
 from jax.sharding import PartitionSpec as P
 
 EX_DEV = 16
@@ -19,7 +23,24 @@
     return (ids[:, None] == jnp.arange(count, dtype=jnp.int32)[None, :]).astype(jnp.float32)
 
 
-def local(
+def scores_from(projected, train_rows, rank, example_ids, query_ids):
+    sketches = sketch_from(
+        projected[:train_rows, :rank],
+        projected[:train_rows, rank:],
+        member_table(example_ids[0], EX_DEV),
+    )
+    query_part = projected[train_rows:]
+    query_table = member_table(query_ids[0], QEX_DEV)
+    local_sketch = sketch_from(query_part[:, :rank], query_part[:, rank:], query_table)
+    query_sketches = lax.all_gather(local_sketch, "dp", axis=0, tiled=True)
+    train_norm = jnp.sqrt(jnp.sum(sketches * sketches, axis=1) + 1e-06)
+    query_norm = jnp.sqrt(jnp.sum(query_sketches * query_sketches, axis=1) + 1e-06)
+    inner = jnp.dot(sketches, query_sketches.T, precision=lax.Precision.HIGHEST)
+    scores = rank * inner / (train_norm[:, None] * query_norm[None, :])
+    return (sketches, scores)
+
+
+def generic_local(
     inputs,
     out_grads,
     example_ids,
@@ -56,25 +77,243 @@
         1,
     )
     projected = lax.psum(partial_sum, "tensor")
+    return scores_from(projected, inputs.shape[0], in_project.shape[0], example_ids, query_ids)
+
+
+CHUNK = 256
+MESH = pl.DeviceIdType.MESH
+
+
+def hidden_kernel(
+    n_tensor, chunks, x_ref, qx_ref, wg_ref, wu_ref, proj_ref, out_ref,
+    tok, wts, lx, lw, zs, zr, ys, yr, xs, xr, ss, sr, fs, fr,
+):
+    group = lax.axis_index("groups")
+    dp = lax.axis_index("dp")
+    me = lax.axis_index("tensor")
+    train, cols = x_ref.shape
+    rows = wg_ref.shape[0]
+    base = group * (chunks * CHUNK)
+    sibling = dp + 1 - 2 * (dp % 2)
+    across = (dp + 2) % 4
+    far = (sibling + 2) % 4
+
+    def tok_at(slot, shard):
+        return tok.at[slot, :, pl.ds(pl.multiple_of(shard * cols, cols), cols)]
+
+    def wts_at(i, quarter):
+        return wts.at[i, pl.ds(pl.multiple_of(quarter * rows, rows), rows), :]
+
+    def z_copy(shard, way, to):
+        return pltpu.make_async_remote_copy(
+            tok_at(0, shard), tok_at(0, shard), zs.at[way, shard], zr.at[shard],
+            device_id={"tensor": to}, device_id_type=MESH)
+
+    def y_copy(shard):
+        return pltpu.make_async_remote_copy(
+            tok_at(0, shard), tok_at(1, shard), ys.at[shard], yr.at[shard],
+            device_id={"groups": 1 - group}, device_id_type=MESH)
+
+    def w_copy(i, quarter, send, recv, to):
+        return pltpu.make_async_remote_copy(
+            wts_at(i, quarter), wts_at(i, quarter), send.at[i], recv.at[i],
+            device_id={"dp": to}, device_id_type=MESH)
+
+    def local_w(i):
+        columns = pl.ds(pl.multiple_of(base + i * CHUNK, CHUNK // 2), CHUNK)
+        mine = pl.ds(pl.multiple_of(dp * rows, rows), rows)
+        return (
+            pltpu.make_async_copy(wg_ref.at[:, columns], wts.at[i, mine, pl.ds(0, CHUNK)], lw.at[0, i]),
+            pltpu.make_async_copy(wu_ref.at[:, columns], wts.at[i, mine, pl.ds(CHUNK, CHUNK)], lw.at[1, i]),
+        )
+
+    own = pl.ds(pl.multiple_of(me * cols, cols), cols)
+    local_x = (
+        pltpu.make_async_copy(x_ref, tok.at[0, pl.ds(0, train), own], lx.at[0]),
+        pltpu.make_async_copy(qx_ref, tok.at[0, pl.ds(train, qx_ref.shape[0]), own], lx.at[1]),
+    )
+    for copy in local_x:
+        copy.start()
+
+    @pl.loop(0, chunks)
+    def _(i):
+        for copy in local_w(i):
+            copy.start()
+
+    barrier = pltpu.get_barrier_semaphore()
+    for target in ({"dp": sibling}, {"dp": across}, {"groups": 1 - group}):
+        pl.semaphore_signal(barrier, inc=1, device_id=target, device_id_type=MESH)
+
+    @pl.when(me > 0)
+    def _():
+        pl.semaphore_signal(barrier, inc=1, device_id={"tensor": me - 1}, device_id_type=MESH)
+
+    @pl.when(me < n_tensor - 1)
+    def _():
+        pl.semaphore_signal(barrier, inc=1, device_id={"tensor": me + 1}, device_id_type=MESH)
+
+    pl.semaphore_wait(barrier, 3 + (me + n_tensor - 1) // n_tensor + (2 * n_tensor - 2 - me) // n_tensor)
+
+    for copy in local_x:
+        copy.wait()
+
+    def pass_right(shard):
+        @pl.when(me < n_tensor - 1)
+        def _():
+            z_copy(shard, 0, me + 1).start()
+
+    def pass_left(shard):
+        @pl.when(me > 0)
+        def _():
+            z_copy(shard, 1, me - 1).start()
+
+    pass_right(me)
+    pass_left(me)
+    y_copy(me).start()
+
+    @pl.loop(0, chunks)
+    def _(i):
+        for copy in local_w(i):
+            copy.wait()
+        w_copy(i, dp, xs, xr, across).start()
+        w_copy(i, dp, ss, sr, sibling).start()
+
+    out_ref[...] = jnp.zeros_like(out_ref)
+
+    def hop(h):
+        @pl.when(me >= h)
+        def _():
+            z_copy(me - h, 0, me).wait_recv()
+            pass_right(me - h)
+            y_copy(me - h).start()
+
+        @pl.when(me + h < n_tensor)
+        def _():
+            z_copy(me + h, 1, me).wait_recv()
+            pass_left(me + h)
+            y_copy(me + h).start()
+
+    def hand_on(i):
+        w_copy(i, across, xs, xr, across).wait_recv()
+        w_copy(i, across, fs, fr, sibling).start()
+
+    def arrive(i):
+        w_copy(i, sibling, ss, sr, sibling).wait_recv()
+        w_copy(i, far, fs, fr, sibling).wait_recv()
+
+    def work(slot, i):
+        both = jnp.dot(tok[slot], wts[i], preferred_element_type=jnp.float32)
+        gate, up = both[:, :CHUNK], both[:, CHUNK:]
+        hidden = (gate / (1.0 + jnp.exp(-gate)) * up).astype(jnp.bfloat16)
+        part = proj_ref[:, pl.ds(pl.multiple_of(base + i * CHUNK, CHUNK // 2), CHUNK)]
+        out_ref[slot] += lax.dot_general(
+            hidden, part, (((1,), (1,)), ((), ())), preferred_element_type=jnp.float32)
+
+    early = chunks // 2 + 1
+    done = 0
+    for h in range(1, n_tensor):
+        upto = max(done, min(early, (early * h) // (n_tensor - 1)))
+        for i in range(done, upto):
+            hand_on(i)
+        done = upto
+        hop(h)
+
+    @pl.loop(0, chunks - 1)
+    def _(i):
+        @pl.when(i >= early)
+        def _():
+            hand_on(i)
+
+        arrive(i)
+        work(0, i)
+
+    @pl.loop(0, n_tensor)
+    def _(shard):
+        y_copy(shard).wait_recv()
+
+    @pl.loop(0, chunks + 1)
+    def _(i):
+        @pl.when(i == chunks - 1)
+        def _():
+            hand_on(chunks - 1)
+            arrive(chunks - 1)
+
+        work(1 - i // chunks, i - i // chunks)
+
+    @pl.loop(0, chunks)
+    def _(i):
+        w_copy(i, dp, xs, xr, across).wait_send()
+        w_copy(i, dp, ss, sr, sibling).wait_send()
+        w_copy(i, across, fs, fr, sibling).wait_send()
+
+    for shard in range(n_tensor):
+        y_copy(shard).wait_send()
+
+        @pl.when((shard <= me) & (me < n_tensor - 1))
+        def _():
+            z_copy(shard, 0, me).wait_send()
+
+        @pl.when((shard >= me) & (me > 0))
+        def _():
+            z_copy(shard, 1, me).wait_send()
+
+
+def hidden_products(n_tensor, inputs, query_inputs, w_gate, w_up, in_project):
+    tokens = inputs.shape[0] + query_inputs.shape[0]
     rank = in_project.shape[0]
-    train_rows = inputs.shape[0]
-    sketches = sketch_from(
-        projected[:train_rows, :rank],
-        projected[:train_rows, rank:],
-        member_table(example_ids[0], EX_DEV),
-    )
-    query_part = projected[train_rows:]
-    query_table = member_table(query_ids[0], QEX_DEV)
-    local_sketch = sketch_from(query_part[:, :rank], query_part[:, rank:], query_table)
-    query_sketches = lax.all_gather(local_sketch, "dp", axis=0, tiled=True)
-    train_norm = jnp.sqrt(jnp.sum(sketches * sketches, axis=1) + 1e-06)
-    query_norm = jnp.sqrt(jnp.sum(query_sketches * query_sketches, axis=1) + 1e-06)
-    inner = jnp.dot(sketches, query_sketches.T, precision=lax.Precision.HIGHEST)
-    scores = rank * inner / (train_norm[:, None] * query_norm[None, :])
-    return (sketches, scores)
+    rows, units = w_gate.shape
+    chunks = units // 2 // CHUNK
+    anywhere = pl.BlockSpec(memory_space=pl.ANY)
+    vmem = pl.BlockSpec(memory_space=pltpu.VMEM)
+    dma = pltpu.SemaphoreType.DMA
+    return pl.pallas_call(
+        functools.partial(hidden_kernel, n_tensor, chunks),
+        out_shape=jax.ShapeDtypeStruct((2, tokens, rank), jnp.float32),
+        in_specs=[anywhere] * 4 + [vmem],
+        out_specs=vmem,
+        scratch_shapes=[
+            pltpu.VMEM((2, tokens, inputs.shape[1] * n_tensor), jnp.bfloat16),
+            pltpu.VMEM((chunks, rows * 4, 2 * CHUNK), jnp.bfloat16),
+            dma((2,)), dma((2, chunks)), dma((2, n_tensor)), dma((n_tensor,)),
+            dma((n_tensor,)), dma((n_tensor,)),
+        ] + [dma((chunks,))] * 6,
+        compiler_params=pltpu.CompilerParams(
+            collective_id=0, has_side_effects=True, vmem_limit_bytes=60 * 2**20),
+        name="hidden_products",
+    )(inputs, query_inputs, w_gate, w_up, in_project)
+
+
+def fused_local(
+    n_tensor,
+    inputs,
+    out_grads,
+    example_ids,
+    query_inputs,
+    query_grads,
+    query_ids,
+    w_gate,
+    w_up,
+    in_project,
+    out_project,
+):
+    right = hidden_products(n_tensor, inputs, query_inputs, w_gate, w_up, in_project)
+    all_grads = jnp.concatenate([out_grads, query_grads], 0)
+    left = jnp.dot(all_grads, out_project.T, preferred_element_type=jnp.float32)
+    right_own = right[0] + lax.ppermute(right[1], "groups", [(0, 1), (1, 0)])
+    projected = lax.psum(jnp.concatenate([left, right_own], 1), "tensor")
+    return scores_from(projected, inputs.shape[0], in_project.shape[0], example_ids, query_ids)
 
 
 def solution(mesh):
+    n_tensor = mesh.shape["tensor"]
+    paired = mesh.shape["groups"] == 2 and mesh.shape["dp"] == 4
+
+    def local(*args):
+        w_gate = args[6]
+        if paired and w_gate.shape[1] % (2 * CHUNK) == 0:
+            return fused_local(n_tensor, *args)
+        return generic_local(*args)
+
     in_specs = (
         P(("groups", "dp"), "tensor"),
         P(("groups", "dp"), "tensor"),

time: 602 us -> 270 us (0.45)
  waiting for transfers between devices: 499 us -> 58.1 us
  Pallas kernels: 0 us -> 181 us
  matrix products: 73.5 us -> 7.5 us
  local copies, waits for them, and re-layouts: 11.1 us -> 3.61 us
    all_gather x5 -> x1, waiting for transfers between devices: 460 us -> 13.2 us  [scores_from(): query_sketches = lax.all_gather(local_sketch, 'dp', axis=0, tiled=True)]
    pallas_call x0 -> x1, Pallas kernels: none -> 181 us  [hidden_products(): pl.pallas_call(functools.partial(hidden_kernel, n_tensor, chunks), out_sh...]
    dot_general x4 -> x2, matrix products: 68.6 us -> 3.32 us  [the longest x1 2.77 us: scores_from(): inner = jnp.dot(sketches, query_sketches.T, precision=lax.Precision.HIGHEST)]
    ppermute x0 -> x1, waiting for transfers between devices: none -> 7.35 us  [fused_local(): right_own = right[0] + lax.ppermute(right[1], 'groups', [(0, 1), (1, 0)])]
  transfers between devices with their start and end apart: 6 -> 3, of which waited for: 6 -> 3; matrix products, arithmetic and copies ran while one was open for 7% -> 1% of each run, Pallas kernels for 0% -> 0%
where the time goes in v1:
time: 270 us; the launch traced here: 269 us
  Pallas kernels  181 us (67%)
  waiting for transfers between devices  58.1 us (22%)
  between operations  14.2 us (5%)
  matrix products  7.5 us (3%)
  local copies, waits for them, and re-layouts  3.61 us (1%)
  other arithmetic  2.85 us (1%)
    pallas_call x1, Pallas kernels, hidden_products(): pl.pallas_call(functools.partial(hidden_kernel, n_tensor, chunks), out_sh...  181 us
    psum x1, waiting for transfers between devices, fused_local(): projected = lax.psum(jnp.concatenate([left, right_own], 1), 'tensor')  37.5 us
    all_gather x1, waiting for transfers between devices, scores_from(): query_sketches = lax.all_gather(local_sketch, 'dp', axis=0, tiled=True)  13.2 us
    ppermute x1, waiting for transfers between devices, fused_local(): right_own = right[0] + lax.ppermute(right[1], 'groups', [(0, 1), (1, 0)])  7.35 us
  transfers between devices with their start and end apart: 3, of which 3 were waited for; matrix products, arithmetic and copies ran while one was open for 1% of the time, Pallas kernels for 0%

profile of v1, /device:TPU:0, one launch (start us, length us, event | category | flops | bytes accessed | tf_op | source)
XLA Modules:
  0.0 269.4 jit_solution(14875707923008950924)
XLA Ops:
  7.2 0.0 all-reduce.2.cloned.1.call-start
  7.2 181.4 %hidden_products.1 = f32[2,768,64]{2,1,0:T(8,128)} custom-call(bf16[512,1024]{1,0:T(8,128)(2,1)} %x_ref.1, bf16[256,1024]{1,0:T(8,128)(2,1)} %qx_ref.1, bf16[1024,3584]{1,0:T(8,128)(2,1)} %wg_ref.1, bf16[1024,3584]{1,0:T(8,128)(2,1)} %wu_ref.1, bf16[64,3584]{1,0:T(8,128)(2,1)} %proj_ref.1), custom_call_target="tpu_custom_call" | custom-call | tf_op jit(solution)/shard_map/hidden_products/pallas_call | solution.py:269
  188.7 1.1 slice_bitcast_fusion
  189.8 1.6 collective-permute-start
  191.4 0.6 fusion
  191.9 7.3 %collective-permute-done = f32[768,64]{1,0:T(8,128)S(1)} collective-permute-done((f32[768,64]{1,0:T(8,128)S(1)}, f32[768,64]{1,0:T(8,128)S(1)}, u32[]{:S(2)}, u32[]{:S(2)}) %collective-permute-start) | collective-permute-done | bytes 196640 | tf_op jit(solution)/shard_map/ppermute | solution.py:302
  199.3 0.9 pad_maximum_fusion
  200.3 0.0 all-gather.2.cloned.1.call-start
  200.3 37.5 %all-reduce.2.cloned.1.call-done = f32[768,128]{1,0:T(8,128)} async-done(((f32[768,128]{1,0:T(8,128)}), f32[768,128]{1,0:T(8,128)}) %all-reduce.2.cloned.1.call-update) | async-done | bytes 393232 | tf_op jit(solution)/shard_map/psum | solution.py:303
  237.8 0.9 slice.29
  238.8 0.1 copy.21
  238.9 0.1 broadcast_multiply_fusion.1
  239.0 2.0 fusion.7
  240.9 0.9 reshape.80
  241.9 0.1 copy.19
  242.0 0.3 broadcast_multiply_fusion
  242.3 2.2 multiply_reduce_fusion.1
  244.5 0.2 copy.20
  244.7 0.2 reshape.79
  244.9 0.1 reduce_sum.26
  245.0 0.1 reduce_sum.27
  245.1 13.2 %all-gather.2.cloned.1.call-done = f32[64,4096]{1,0:T(8,128)} async-done(((f32[16,4096]{1,0:T(8,128)}), f32[64,4096]{1,0:T(8,128)}) %all-gather.2.cloned.1.call-update) | async-done | bytes 1048592 | tf_op jit(solution)/shard_map/all_gather | solution.py:35
  258.3 1.4 multiply_reduce_fusion
  259.8 2.8 %fusion.4 = f32[16,64]{1,0:T(8,128)} fusion(f32[16,4096]{1,0:T(8,128)S(1)} %reshape.79, f32[64,4096]{1,0:T(8,128)} %all-gather.2.cloned.1.call-done, f32[64]{0:T(128)S(1)} %add_sqrt_fusion, f32[16]{0:T(128)S(1)} %add_sqrt_fusion.1), kind=kOutput, calls=%fused_computation.5 | convolution fusion | flops 50334720 | bytes 1315136 | tf_op jit(solution)/shard_map/dot_general | solution.py:38
  (24 shorter events, 0.2 us)
Async XLA Ops:
  7.2 184.2 %copy-start = (bf16[64,1024]{1,0:T(8,128)(2,1)S(1)}, bf16[64,1024]{1,0:T(8,128)(2,1)}, u32[]{:S(2)}) copy-start(bf16[64,1024]{1,0:T(8,128)(2,1)} %param.19) | copy-start | bytes 393220
  7.2 184.2 %copy-start.6 = (bf16[512,1024]{1,0:T(8,128)(2,1)S(1)}, bf16[512,1024]{1,0:T(8,128)(2,1)}, u32[]{:S(2)}) copy-start(bf16[512,1024]{1,0:T(8,128)(2,1)} %param.11) | copy-start | bytes 3145732
  7.2 184.2 %copy-start.7 = (bf16[256,1024]{1,0:T(8,128)(2,1)S(1)}, bf16[256,1024]{1,0:T(8,128)(2,1)}, u32[]{:S(2)}) copy-start(bf16[256,1024]{1,0:T(8,128)(2,1)} %param.14) | copy-start | bytes 1572868
  7.2 230.6 %all-reduce.2.cloned.1.call-start = ((), (), s32[]{:S(2)}) async-start(), calls=%async_computation | async-start | bytes 786432 | tf_op jit(solution)/shard_map/psum | solution.py:303
  188.6 10.6 %copy-start.1 = (f32[2,768,64]{2,1,0:T(8,128)S(1)}, f32[2,768,64]{2,1,0:T(8,128)}, u32[]{:S(2)}) copy-start(f32[2,768,64]{2,1,0:T(8,128)} %hidden_products.1) | copy-start | bytes 1179652
  189.8 9.5 %collective-permute-start = (f32[768,64]{1,0:T(8,128)S(1)}, f32[768,64]{1,0:T(8,128)S(1)}, u32[]{:S(2)}, u32[]{:S(2)}) collective-permute-start(f32[768,64]{1,0:T(8,128)S(1)} %slice_bitcast_fusion), channel_id=1, source_target_pairs={{0,16},{16,0},{1,17},{17,1},{2,18},{18,2},{3,19},{19,3},{4,20},{20... | collective-permute-start | bytes 589832 | tf_op jit(solution)/shard_map/ppermute | solution.py:302
  191.9 8.4 %copy-start.5 = (s32[1,256]{1,0:T(1,128)S(1)}, s32[1,256]{1,0:T(1,128)}, u32[]{:S(2)}) copy-start(s32[1,256]{1,0:T(1,128)} %param.15) | copy-start | bytes 3076
  200.3 58.1 %all-gather.2.cloned.1.call-start = ((), (), s32[]{:S(2)}) async-start(), calls=%async_computation.1 | async-start | bytes 1310720 | tf_op jit(solution)/shard_map/all_gather | solution.py:35
  238.8 3.1 %copy-start.4 = (s32[1,512]{1,0:T(1,128)S(1)}, s32[1,512]{1,0:T(1,128)}, u32[]{:S(2)}) copy-start(s32[1,512]{1,0:T(1,128)} %param.12) | copy-start | bytes 6148
  238.8 3.1 %copy-start.2 = (f32[768,128]{1,0:T(8,128)S(1)}, f32[768,128]{1,0:T(8,128)}, u32[]{:S(2)}) copy-start(f32[768,128]{1,0:T(8,128)} %all-reduce.2.cloned.1.call-done) | copy-start | bytes 1179652
  244.9 17.6 %copy-start.3 = (f32[16,4096]{1,0:T(8,128)}, f32[16,4096]{1,0:T(8,128)S(1)}, u32[]{:S(2)}) copy-start(f32[16,4096]{1,0:T(8,128)S(1)} %reshape.79) | copy-start | bytes 786436
Sparse Core Ops, SparseCore 0:
  200.4 37.4 all-reduce.1
  242.0 16.3 all-gather.1

commit v2 on v1

--- a/solution.py
+++ b/solution.py
@@ -33,11 +33,15 @@
     query_table = member_table(query_ids[0], QEX_DEV)
     local_sketch = sketch_from(query_part[:, :rank], query_part[:, rank:], query_table)
     query_sketches = lax.all_gather(local_sketch, "dp", axis=0, tiled=True)
+    return sketches, scores_of(sketches, query_sketches, rank)
+
+
+def scores_of(sketches, query_sketches, rank):
     train_norm = jnp.sqrt(jnp.sum(sketches * sketches, axis=1) + 1e-06)
     query_norm = jnp.sqrt(jnp.sum(query_sketches * query_sketches, axis=1) + 1e-06)
     inner = jnp.dot(sketches, query_sketches.T, precision=lax.Precision.HIGHEST)
     scores = rank * inner / (train_norm[:, None] * query_norm[None, :])
-    return (sketches, scores)
+    return scores
 
 
 def generic_local(
@@ -84,9 +88,11 @@
 MESH = pl.DeviceIdType.MESH
 
 
-def hidden_kernel(
-    n_tensor, chunks, x_ref, qx_ref, wg_ref, wu_ref, proj_ref, out_ref,
-    tok, wts, lx, lw, zs, zr, ys, yr, xs, xr, ss, sr, fs, fr,
+def sketch_kernel(
+    n_tensor, chunks, x_ref, qx_ref, wg_ref, wu_ref, dy_ref, qdy_ref, proj_ref, oproj_ref, ids_ref, qids_ref,
+    sketch_ref, queries_ref,
+    tok, wts, grads, acc, lefts, swap, parts, terms, whole,
+    lx, lw, zs, zr, ys, yr, xs, xr, ss, sr, fs, fr, lg, ls, lr, ps, pr, ts, tr, ws, wr, qs, qr,
 ):
     group = lax.axis_index("groups")
     dp = lax.axis_index("dp")
@@ -132,6 +138,10 @@
         pltpu.make_async_copy(x_ref, tok.at[0, pl.ds(0, train), own], lx.at[0]),
         pltpu.make_async_copy(qx_ref, tok.at[0, pl.ds(train, qx_ref.shape[0]), own], lx.at[1]),
     )
+    local_g = (
+        pltpu.make_async_copy(dy_ref, grads.at[pl.ds(0, train)], lg.at[0]),
+        pltpu.make_async_copy(qdy_ref, grads.at[pl.ds(train, qdy_ref.shape[0])], lg.at[1]),
+    )
     for copy in local_x:
         copy.start()
 
@@ -141,18 +151,14 @@
             copy.start()
 
     barrier = pltpu.get_barrier_semaphore()
-    for target in ({"dp": sibling}, {"dp": across}, {"groups": 1 - group}):
+    targets = [{"groups": 1 - group}]
+    targets += [{"dp": (dp + step) % 4} for step in range(1, 4)]
+    targets += [{"tensor": (me + step) % n_tensor} for step in range(1, n_tensor)]
+    for target in targets:
         pl.semaphore_signal(barrier, inc=1, device_id=target, device_id_type=MESH)
-
-    @pl.when(me > 0)
-    def _():
-        pl.semaphore_signal(barrier, inc=1, device_id={"tensor": me - 1}, device_id_type=MESH)
-
-    @pl.when(me < n_tensor - 1)
-    def _():
-        pl.semaphore_signal(barrier, inc=1, device_id={"tensor": me + 1}, device_id_type=MESH)
-
-    pl.semaphore_wait(barrier, 3 + (me + n_tensor - 1) // n_tensor + (2 * n_tensor - 2 - me) // n_tensor)
+    for copy in local_g:
+        copy.start()
+    pl.semaphore_wait(barrier, len(targets))
 
     for copy in local_x:
         copy.wait()
@@ -178,7 +184,11 @@
         w_copy(i, dp, xs, xr, across).start()
         w_copy(i, dp, ss, sr, sibling).start()
 
-    out_ref[...] = jnp.zeros_like(out_ref)
+    acc[...] = jnp.zeros_like(acc)
+    for copy in local_g:
+        copy.wait()
+    lefts[me] = lax.dot_general(
+        oproj_ref[...], grads[...], (((1,), (1,)), ((), ())), preferred_element_type=jnp.float32)
 
     def hop(h):
         @pl.when(me >= h)
@@ -206,7 +216,7 @@
         gate, up = both[:, :CHUNK], both[:, CHUNK:]
         hidden = (gate / (1.0 + jnp.exp(-gate)) * up).astype(jnp.bfloat16)
         part = proj_ref[:, pl.ds(pl.multiple_of(base + i * CHUNK, CHUNK // 2), CHUNK)]
-        out_ref[slot] += lax.dot_general(
+        acc[slot] += lax.dot_general(
             hidden, part, (((1,), (1,)), ((), ())), preferred_element_type=jnp.float32)
 
     early = chunks // 2 + 1
@@ -218,6 +228,36 @@
         done = upto
         hop(h)
 
+    def others():
+        return [(me + step) % n_tensor for step in range(1, n_tensor)]
+
+    def left_copy(source, to):
+        return pltpu.make_async_remote_copy(
+            lefts.at[source], lefts.at[source], ls.at[to], lr.at[source],
+            device_id={"tensor": to}, device_id_type=MESH)
+
+    def swap_copy():
+        return pltpu.make_async_remote_copy(
+            swap.at[0], swap.at[1], ps.at[0], pr.at[0], device_id={"groups": 1 - group}, device_id_type=MESH)
+
+    def term_copy(source, to):
+        return pltpu.make_async_remote_copy(
+            parts.at[to], terms.at[source], ts.at[to], tr.at[source],
+            device_id={"tensor": to}, device_id_type=MESH)
+
+    def whole_copy(source, to):
+        return pltpu.make_async_remote_copy(
+            whole.at[source], whole.at[source], ws.at[to], wr.at[source],
+            device_id={"tensor": to}, device_id_type=MESH)
+
+    def query_copy(source, to):
+        return pltpu.make_async_remote_copy(
+            queries_ref.at[source], queries_ref.at[source], qs.at[to], qr.at[source],
+            device_id={"dp": to}, device_id_type=MESH)
+
+    for to in others():
+        left_copy(me, to).start()
+
     @pl.loop(0, chunks - 1)
     def _(i):
         @pl.when(i >= early)
@@ -231,14 +271,71 @@
     def _(shard):
         y_copy(shard).wait_recv()
 
-    @pl.loop(0, chunks + 1)
+    @pl.loop(0, chunks - 1)
     def _(i):
-        @pl.when(i == chunks - 1)
-        def _():
-            hand_on(chunks - 1)
-            arrive(chunks - 1)
-
-        work(1 - i // chunks, i - i // chunks)
+        work(1, i)
+
+    hand_on(chunks - 1)
+    arrive(chunks - 1)
+    half = tok.shape[1] // 2
+    rank = proj_ref.shape[0]
+
+    def packed(slot):
+        return jnp.concatenate([acc[slot, :half], acc[slot, half:]], axis=1)
+
+    @pl.loop(0, 2)
+    def _(turn):
+        work(1 - turn, chunks - 1)
+
+        @pl.when(turn == 0)
+        def _():
+            swap[0] = packed(1)
+            swap_copy().start()
+
+    swap_copy().wait_recv()
+    parts[...] = (packed(0) + swap[1]).reshape(parts.shape)
+    for to in others():
+        term_copy(me, to).start()
+    total = parts[me]
+    for source in others():
+        term_copy(source, source).wait_recv()
+        total = total + terms[source]
+    whole[me] = total
+    for to in others():
+        whole_copy(me, to).start()
+    for source in others():
+        left_copy(source, source).wait_recv()
+    left = lefts[0]
+    for source in range(1, n_tensor):
+        left = left + lefts[source]
+    for source in others():
+        whole_copy(source, source).wait_recv()
+    both = whole[...].reshape(half, 2 * rank)
+    right = jnp.concatenate([both[:, :rank], both[:, rank:]], axis=0)
+
+    def outer_sums(left, right, ids, count):
+        sums = []
+        for side in range(2):
+            some = left[side * (rank // 2):(side + 1) * (rank // 2)]
+            spread = jnp.concatenate([jnp.where(ids == e, some, 0.0) for e in range(count)], axis=0)
+            sums.append(jnp.dot(
+                spread, right, precision=lax.Precision.HIGHEST, preferred_element_type=jnp.float32))
+        return jnp.concatenate(sums, axis=1)
+
+    queries_ref[dp] = outer_sums(left[:, train:], right[train:], qids_ref[...], QEX_DEV)
+    for step in range(1, 4):
+        query_copy(dp, (dp + step) % 4).start()
+    sketch_ref[...] = outer_sums(left[:, :train], right[:train], ids_ref[...], EX_DEV)
+    for step in range(1, 4):
+        query_copy((dp + step) % 4, (dp + step) % 4).wait_recv()
+
+    for to in others():
+        left_copy(me, to).wait_send()
+        term_copy(me, to).wait_send()
+        whole_copy(me, to).wait_send()
+    swap_copy().wait_send()
+    for step in range(1, 4):
+        query_copy(dp, (dp + step) % 4).wait_send()
 
     @pl.loop(0, chunks)
     def _(i):
@@ -258,7 +355,9 @@
             z_copy(shard, 1, me).wait_send()
 
 
-def hidden_products(n_tensor, inputs, query_inputs, w_gate, w_up, in_project):
+def sketch_products(
+    n_tensor, inputs, out_grads, example_ids, query_inputs, query_grads, query_ids, w_gate, w_up, in_project, out_project
+):
     tokens = inputs.shape[0] + query_inputs.shape[0]
     rank = in_project.shape[0]
     rows, units = w_gate.shape
@@ -266,42 +365,44 @@
     anywhere = pl.BlockSpec(memory_space=pl.ANY)
     vmem = pl.BlockSpec(memory_space=pltpu.VMEM)
     dma = pltpu.SemaphoreType.DMA
+    f32 = jnp.float32
     return pl.pallas_call(
-        functools.partial(hidden_kernel, n_tensor, chunks),
-        out_shape=jax.ShapeDtypeStruct((2, tokens, rank), jnp.float32),
-        in_specs=[anywhere] * 4 + [vmem],
-        out_specs=vmem,
+        functools.partial(sketch_kernel, n_tensor, chunks),
+        out_shape=(
+            jax.ShapeDtypeStruct((EX_DEV * rank // 2, 2 * rank), f32),
+            jax.ShapeDtypeStruct((4, QEX_DEV * rank // 2, 2 * rank), f32),
+        ),
+        in_specs=[anywhere] * 6 + [vmem] * 4,
+        out_specs=(vmem, vmem),
         scratch_shapes=[
             pltpu.VMEM((2, tokens, inputs.shape[1] * n_tensor), jnp.bfloat16),
             pltpu.VMEM((chunks, rows * 4, 2 * CHUNK), jnp.bfloat16),
+            pltpu.VMEM((tokens, out_grads.shape[1]), jnp.bfloat16),
+            pltpu.VMEM((2, tokens, rank), f32),
+            pltpu.VMEM((n_tensor, rank, tokens), f32),
+            pltpu.VMEM((2, tokens // 2, 2 * rank), f32),
+            pltpu.VMEM((n_tensor, tokens // 2 // n_tensor, 2 * rank), f32),
+            pltpu.VMEM((n_tensor, tokens // 2 // n_tensor, 2 * rank), f32),
+            pltpu.VMEM((n_tensor, tokens // 2 // n_tensor, 2 * rank), f32),
             dma((2,)), dma((2, chunks)), dma((2, n_tensor)), dma((n_tensor,)),
             dma((n_tensor,)), dma((n_tensor,)),
-        ] + [dma((chunks,))] * 6,
+        ] + [dma((chunks,))] * 6 + [dma((2,))] + [dma((n_tensor,))] * 2 + [dma((1,))] * 2
+        + [dma((n_tensor,))] * 4 + [dma((4,))] * 2,
         compiler_params=pltpu.CompilerParams(
             collective_id=0, has_side_effects=True, vmem_limit_bytes=60 * 2**20),
-        name="hidden_products",
-    )(inputs, query_inputs, w_gate, w_up, in_project)
-
-
-def fused_local(
-    n_tensor,
-    inputs,
-    out_grads,
-    example_ids,
-    query_inputs,
-    query_grads,
-    query_ids,
-    w_gate,
-    w_up,
-    in_project,
-    out_project,
-):
-    right = hidden_products(n_tensor, inputs, query_inputs, w_gate, w_up, in_project)
-    all_grads = jnp.concatenate([out_grads, query_grads], 0)
-    left = jnp.dot(all_grads, out_project.T, preferred_element_type=jnp.float32)
-    right_own = right[0] + lax.ppermute(right[1], "groups", [(0, 1), (1, 0)])
-    projected = lax.psum(jnp.concatenate([left, right_own], 1), "tensor")
-    return scores_from(projected, inputs.shape[0], in_project.shape[0], example_ids, query_ids)
+        name="sketch_products",
+    )(inputs, query_inputs, w_gate, w_up, out_grads, query_grads, in_project, out_project, example_ids, query_ids)
+
+
+def fused_local(n_tensor, *args):
+    train, queries = sketch_products(n_tensor, *args)
+    rank = args[8].shape[0]
+
+    def unpacked(pairs):
+        return pairs.reshape(-1, rank // 2, 2, rank).transpose(0, 2, 1, 3).reshape(-1, rank * rank)
+
+    sketches = unpacked(train)
+    return sketches, scores_of(sketches, unpacked(queries), rank)
 
 
 def solution(mesh):

time: 270 us -> 217 us (0.80)
  waiting for transfers between devices: 58.1 us -> 0 us
  Pallas kernels: 181 us -> 205 us
  between operations: 14.2 us -> 0.67 us
  matrix products: 7.5 us -> 3.67 us
    psum x1 -> x0, waiting for transfers between devices: 37.5 us -> none  [fused_local(): projected = lax.psum(jnp.concatenate([left, right_own], 1), 'tensor')]
    pallas_call x1, Pallas kernels: 181 us -> 205 us  [sketch_products(): pl.pallas_call(functools.partial(sketch_kernel, n_tensor, chunks), out_sh...]
    all_gather x1 -> x0, waiting for transfers between devices: 13.2 us -> none  [scores_from(): query_sketches = lax.all_gather(local_sketch, 'dp', axis=0, tiled=True)]
    ppermute x1 -> x0, waiting for transfers between devices: 7.35 us -> none  [fused_local(): right_own = right[0] + lax.ppermute(right[1], 'groups', [(0, 1), (1, 0)])]
    dot_general x4 -> x1, matrix products: 7.5 us -> 3.67 us  [scores_of(): inner = jnp.dot(sketches, query_sketches.T, precision=lax.Precision.HIGHEST)]
    reshape x2 -> x3, local copies, waits for them, and re-layouts: 1.07 us -> 4.83 us  [unpacked(): pairs.reshape(-1, rank // 2, 2, rank).transpose(0, 2, 1, 3)]
  transfers between devices with their start and end apart: 3 -> 0, of which waited for: 3 -> 0; matrix products, arithmetic and copies ran while one was open for 1% -> 0% of each run, Pallas kernels for 0% -> 0%
where the time goes in v2:
time: 217 us; the launch traced here: 216 us
  Pallas kernels  205 us (94%)
  local copies, waits for them, and re-layouts  4.88 us (2%)
  matrix products  3.67 us (2%)
    pallas_call x1, Pallas kernels, sketch_products(): pl.pallas_call(functools.partial(sketch_kernel, n_tensor, chunks), out_sh...  205 us
    reshape x3, local copies, waits for them, and re-layouts, unpacked(): pairs.reshape(-1, rank // 2, 2, rank).transpose(0, 2, 1, 3)  4.83 us

profile of v2, /device:TPU:0, one launch (start us, length us, event | category | flops | bytes accessed | tf_op | source)
XLA Modules:
  0.0 215.6 jit_solution(13080115439984322527)
XLA Ops:
  0.6 204.7 %sketch_products.1 = (f32[512,128]{1,0:T(8,128)}, f32[4,512,128]{2,1,0:T(8,128)}) custom-call(bf16[512,1024]{1,0:T(8,128)(2,1)} %x_ref.1, bf16[256,1024]{1,0:T(8,128)(2,1)} %qx_ref.1, bf16[1024,3584]{1,0:T(8,128)(2,1)} %wg_ref.1, bf16[1024,3584]{1,0:T(8,128)(2,1)} %wu_ref.1, bf16[512,1024]{1,0:T(8,128)(2,1)} %dy_ref.1, bf16[256,1024]{1,0:T(8,128)(2,1)} %qdy_ref.1, ...), custom_call_target="tpu_custom_call" | custom-call | tf_op jit(solution)/shard_map/sketch_products/pallas_call | solution.py:369
  205.4 1.3 reshape.22
  206.6 0.4 fusion.14
  207.1 2.7 %reshape.24 = f32[64,32,2,64]{3,2,1,0:T(2,128)S(1)} reshape(f32[4,512,128]{2,1,0:T(8,128)} %get-tuple-element.5) | data formatting | bytes 2097152 | tf_op jit(solution)/shard_map/reshape | solution.py:402
  209.7 1.3 fusion.2
  211.0 3.7 %fusion.10 = f32[16,64]{1,0:T(8,128)} fusion(f32[64,32,2,64]{3,2,1,0:T(2,128)S(1)} %reshape.24, f32[16,32,2,64]{3,2,1,0:T(2,128)S(1)} %reshape.22, f32[64]{0:T(128)S(1)} %add_sqrt_fusion, f32[16]{0:T(128)S(1)} %add_sqrt_fusion.1), kind=kOutput, calls=%fused_computation.7 | convolution fusion | flops 50334720 | bytes 1315136 | tf_op jit(solution)/shard_map/dot_general | solution.py:42
  214.7 0.1 copy.34
  214.8 0.9 reshape.23
  (2 shorter events, 0.0 us)

commit v3 on v2

--- a/solution.py
+++ b/solution.py
@@ -90,9 +90,10 @@
 
 def sketch_kernel(
     n_tensor, chunks, x_ref, qx_ref, wg_ref, wu_ref, dy_ref, qdy_ref, proj_ref, oproj_ref, ids_ref, qids_ref,
-    sketch_ref, queries_ref,
+    sketch_ref, scores_ref,
     tok, wts, grads, acc, lefts, swap, parts, terms, whole,
-    lx, lw, zs, zr, ys, yr, xs, xr, ss, sr, fs, fr, lg, ls, lr, ps, pr, ts, tr, ws, wr, qs, qr,
+    halfway, spreads, grams, lqs, rqs, norms, idrows,
+    lx, lw, zs, zr, ys, yr, xs, xr, ss, sr, fs, fr, lg, ls, lr, ps, pr, ts, tr, ws, wr, qs, qr, ns, nr, ds, dr, es, er,
 ):
     group = lax.axis_index("groups")
     dp = lax.axis_index("dp")
@@ -211,13 +212,21 @@
         w_copy(i, sibling, ss, sr, sibling).wait_recv()
         w_copy(i, far, fs, fr, sibling).wait_recv()
 
-    def work(slot, i):
-        both = jnp.dot(tok[slot], wts[i], preferred_element_type=jnp.float32)
+    def finish(slot, i, both):
         gate, up = both[:, :CHUNK], both[:, CHUNK:]
         hidden = (gate / (1.0 + jnp.exp(-gate)) * up).astype(jnp.bfloat16)
         part = proj_ref[:, pl.ds(pl.multiple_of(base + i * CHUNK, CHUNK // 2), CHUNK)]
         acc[slot] += lax.dot_general(
             hidden, part, (((1,), (1,)), ((), ())), preferred_element_type=jnp.float32)
+
+    def work(slot, i):
+        finish(slot, i, jnp.dot(tok[slot], wts[i], preferred_element_type=jnp.float32))
+
+    def side_dot(slot, i, side):
+        return jnp.dot(
+            tok[slot, :, pl.ds(pl.multiple_of(side * (2 * rows), 2 * rows), 2 * rows)],
+            wts[i, pl.ds(pl.multiple_of(side * (2 * rows), 2 * rows), 2 * rows), :],
+            preferred_element_type=jnp.float32)
 
     early = chunks // 2 + 1
     done = 0
@@ -250,11 +259,15 @@
             whole.at[source], whole.at[source], ws.at[to], wr.at[source],
             device_id={"tensor": to}, device_id_type=MESH)
 
-    def query_copy(source, to):
-        return pltpu.make_async_remote_copy(
-            queries_ref.at[source], queries_ref.at[source], qs.at[to], qr.at[source],
+    def dp_copy(buffer, send, recv, source, to):
+        return pltpu.make_async_remote_copy(
+            buffer.at[source], buffer.at[source], send.at[to], recv.at[source],
             device_id={"dp": to}, device_id_type=MESH)
 
+    idrows[dp] = qids_ref[...]
+    elsewhere = [(dp + step) % 4 for step in range(1, 4)]
+    for to in elsewhere:
+        dp_copy(idrows, ds, dr, dp, to).start()
     for to in others():
         left_copy(me, to).start()
 
@@ -267,6 +280,39 @@
         arrive(i)
         work(0, i)
 
+    rank = proj_ref.shape[0]
+    half = tok.shape[1] // 2
+    for source in others():
+        left_copy(source, source).wait_recv()
+    left = lefts[0]
+    for source in range(1, n_tensor):
+        left = left + lefts[source]
+    lqs[dp] = left[:, train:]
+    dp_copy(lqs, es, er, dp, sibling).start()
+    dp_copy(lqs, es, er, dp, across).start()
+
+    def spread(left, ids, count, at, size):
+        for side in range(2):
+            some = left[side * (rank // 2):(side + 1) * (rank // 2)]
+            top = some.astype(jnp.bfloat16).astype(jnp.float32)
+            for k, piece in enumerate((top, some - top)):
+                rows_of = [jnp.where(ids == e, piece, 0.0) for e in range(count)]
+                spreads[k, side, :, pl.ds(at, size)] = jnp.concatenate(rows_of, axis=0).astype(jnp.bfloat16)
+
+    spread(left[:, :train], ids_ref[...], EX_DEV, 0, train)
+    spread(left[:, train:], qids_ref[...], QEX_DEV, train, left.shape[1] - train)
+    dp_copy(lqs, es, er, across, across).wait_recv()
+    far_copy = pltpu.make_async_remote_copy(
+        lqs.at[across], lqs.at[across], es.at[far], er.at[across],
+        device_id={"dp": sibling}, device_id_type=MESH)
+    far_copy.start()
+    dp_copy(lqs, es, er, sibling, sibling).wait_recv()
+    dp_copy(lqs, es, er, far, far).wait_recv()
+    for k in range(4):
+        grams[k] = lax.dot_general(
+            left[:, :train], lqs[k], (((0,), (0,)), ((), ())),
+            precision=lax.Precision.HIGHEST, preferred_element_type=jnp.float32)
+
     @pl.loop(0, n_tensor)
     def _(shard):
         y_copy(shard).wait_recv()
@@ -275,17 +321,22 @@
     def _(i):
         work(1, i)
 
-    hand_on(chunks - 1)
-    arrive(chunks - 1)
-    half = tok.shape[1] // 2
-    rank = proj_ref.shape[0]
+    last = chunks - 1
+    w_copy(last, sibling, ss, sr, sibling).wait_recv()
+
+    @pl.loop(0, 2)
+    def _(slot):
+        halfway[slot] = side_dot(slot, last, dp // 2)
+
+    hand_on(last)
+    w_copy(last, far, fs, fr, sibling).wait_recv()
 
     def packed(slot):
         return jnp.concatenate([acc[slot, :half], acc[slot, half:]], axis=1)
 
     @pl.loop(0, 2)
     def _(turn):
-        work(1 - turn, chunks - 1)
+        finish(1 - turn, last, halfway[1 - turn] + side_dot(1 - turn, last, 1 - dp // 2))
 
         @pl.when(turn == 0)
         def _():
@@ -304,38 +355,86 @@
     for to in others():
         whole_copy(me, to).start()
     for source in others():
-        left_copy(source, source).wait_recv()
-    left = lefts[0]
-    for source in range(1, n_tensor):
-        left = left + lefts[source]
-    for source in others():
         whole_copy(source, source).wait_recv()
     both = whole[...].reshape(half, 2 * rank)
     right = jnp.concatenate([both[:, :rank], both[:, rank:]], axis=0)
 
-    def outer_sums(left, right, ids, count):
+    rqs[dp] = right[train:]
+    for to in elsewhere:
+        dp_copy(rqs, qs, qr, dp, to).start()
+
+    def split(value):
+        top = value.astype(jnp.bfloat16)
+        return top, (value - top.astype(jnp.float32)).astype(jnp.bfloat16)
+
+    def outer_sums(right, at):
+        top, rest = split(right)
+        pair = jnp.concatenate([top, rest], axis=1)
         sums = []
         for side in range(2):
-            some = left[side * (rank // 2):(side + 1) * (rank // 2)]
-            spread = jnp.concatenate([jnp.where(ids == e, some, 0.0) for e in range(count)], axis=0)
-            sums.append(jnp.dot(
-                spread, right, precision=lax.Precision.HIGHEST, preferred_element_type=jnp.float32))
+            span = pl.ds(at, right.shape[0])
+            first = jnp.dot(spreads[0, side, :, span], pair, preferred_element_type=jnp.float32)
+            second = jnp.dot(spreads[1, side, :, span], top, preferred_element_type=jnp.float32)
+            sums.append(first[:, :rank] + first[:, rank:] + second)
         return jnp.concatenate(sums, axis=1)
 
-    queries_ref[dp] = outer_sums(left[:, train:], right[train:], qids_ref[...], QEX_DEV)
-    for step in range(1, 4):
-        query_copy(dp, (dp + step) % 4).start()
-    sketch_ref[...] = outer_sums(left[:, :train], right[:train], ids_ref[...], EX_DEV)
-    for step in range(1, 4):
-        query_copy((dp + step) % 4, (dp + step) % 4).wait_recv()
+    own_queries = outer_sums(right[train:], train)
+    across_lanes = lax.dot_general(
+        jnp.ones((8, 2 * rank), jnp.float32), own_queries * own_queries, (((1,), (1,)), ((), ())),
+        precision=lax.Precision.HIGHEST, preferred_element_type=jnp.float32)
+    entries = own_queries.shape[0]
+    query_of = lax.broadcasted_iota(jnp.int32, (entries, 128), 0) // (entries // QEX_DEV)
+    place = lax.broadcasted_iota(jnp.int32, (entries, 128), 1)
+    norms[dp] = jnp.dot(
+        across_lanes, (query_of == place).astype(jnp.float32),
+        precision=lax.Precision.HIGHEST, preferred_element_type=jnp.float32)
+    for to in elsewhere:
+        dp_copy(norms, ns, nr, dp, to).start()
+
+    sketch = outer_sums(right[:train], 0)
+    sketch_ref[...] = sketch
+    squares = jnp.sum((sketch * sketch).reshape(EX_DEV, sketch.shape[0] // EX_DEV, 2 * rank), axis=1)
+    train_norm = jnp.sqrt(jnp.sum(squares, axis=1, keepdims=True) + 1e-06)
+
+    for source in elsewhere:
+        dp_copy(rqs, qs, qr, source, source).wait_recv()
+        dp_copy(idrows, ds, dr, source, source).wait_recv()
+        dp_copy(norms, ns, nr, source, source).wait_recv()
+
+    def table(ids, count):
+        return (lax.broadcasted_iota(jnp.int32, (count, ids.shape[1]), 0) == ids).astype(jnp.float32)
+
+    examples = table(ids_ref[...], EX_DEV).astype(jnp.bfloat16)
+    top, rest = split(right[:train])
+    mine = jnp.concatenate([top, rest, top], axis=1)
+    found = []
+    for k in range(4):
+        top, rest = split(rqs[k])
+        theirs = jnp.concatenate([top, top, rest], axis=1)
+        gram = grams[k] * lax.dot_general(
+            mine, theirs, (((1,), (1,)), ((), ())), preferred_element_type=jnp.float32)
+        top, rest = split(gram)
+        by_example = jnp.dot(examples, top, preferred_element_type=jnp.float32) + jnp.dot(
+            examples, rest, preferred_element_type=jnp.float32)
+        inner = lax.dot_general(
+            by_example, table(idrows[k], QEX_DEV), (((1,), (1,)), ((), ())),
+            precision=lax.Precision.HIGHEST, preferred_element_type=jnp.float32)
+        query_norm = jnp.sqrt(norms[k][:1, :QEX_DEV] + 1e-06)
+        found.append(rank * inner / (train_norm * query_norm))
+    scores_ref[...] = jnp.concatenate(found, axis=1)
 
     for to in others():
         left_copy(me, to).wait_send()
         term_copy(me, to).wait_send()
         whole_copy(me, to).wait_send()
     swap_copy().wait_send()
-    for step in range(1, 4):
-        query_copy(dp, (dp + step) % 4).wait_send()
+    for to in elsewhere:
+        dp_copy(rqs, qs, qr, dp, to).wait_send()
+        dp_copy(idrows, ds, dr, dp, to).wait_send()
+        dp_copy(norms, ns, nr, dp, to).wait_send()
+    dp_copy(lqs, es, er, dp, sibling).wait_send()
+    dp_copy(lqs, es, er, dp, across).wait_send()
+    far_copy.wait_send()
 
     @pl.loop(0, chunks)
     def _(i):
@@ -370,7 +469,7 @@
         functools.partial(sketch_kernel, n_tensor, chunks),
         out_shape=(
             jax.ShapeDtypeStruct((EX_DEV * rank // 2, 2 * rank), f32),
-            jax.ShapeDtypeStruct((4, QEX_DEV * rank // 2, 2 * rank), f32),
+            jax.ShapeDtypeStruct((EX_DEV, 4 * QEX_DEV), f32),
         ),
         in_specs=[anywhere] * 6 + [vmem] * 4,
         out_specs=(vmem, vmem),
@@ -384,10 +483,17 @@
             pltpu.VMEM((n_tensor, tokens // 2 // n_tensor, 2 * rank), f32),
             pltpu.VMEM((n_tensor, tokens // 2 // n_tensor, 2 * rank), f32),
             pltpu.VMEM((n_tensor, tokens // 2 // n_tensor, 2 * rank), f32),
+            pltpu.VMEM((2, tokens, 2 * CHUNK), f32),
+            pltpu.VMEM((2, 2, EX_DEV * rank // 2, tokens), jnp.bfloat16),
+            pltpu.VMEM((4, inputs.shape[0], query_inputs.shape[0]), f32),
+            pltpu.VMEM((4, rank, query_inputs.shape[0]), f32),
+            pltpu.VMEM((4, query_inputs.shape[0], rank), f32),
+            pltpu.VMEM((4, 8, 128), f32),
+            pltpu.VMEM((4, 1, query_inputs.shape[0]), jnp.int32),
             dma((2,)), dma((2, chunks)), dma((2, n_tensor)), dma((n_tensor,)),
             dma((n_tensor,)), dma((n_tensor,)),
         ] + [dma((chunks,))] * 6 + [dma((2,))] + [dma((n_tensor,))] * 2 + [dma((1,))] * 2
-        + [dma((n_tensor,))] * 4 + [dma((4,))] * 2,
+        + [dma((n_tensor,))] * 4 + [dma((4,))] * 8,
         compiler_params=pltpu.CompilerParams(
             collective_id=0, has_side_effects=True, vmem_limit_bytes=60 * 2**20),
         name="sketch_products",
@@ -395,14 +501,10 @@
 
 
 def fused_local(n_tensor, *args):
-    train, queries = sketch_products(n_tensor, *args)
+    pairs, scores = sketch_products(n_tensor, *args)
     rank = args[8].shape[0]
-
-    def unpacked(pairs):
-        return pairs.reshape(-1, rank // 2, 2, rank).transpose(0, 2, 1, 3).reshape(-1, rank * rank)
-
-    sketches = unpacked(train)
-    return sketches, scores_of(sketches, unpacked(queries), rank)
+    sketches = pairs.reshape(-1, rank // 2, 2, rank).transpose(0, 2, 1, 3).reshape(-1, rank * rank)
+    return sketches, scores
 
 
 def solution(mesh):

time: 217 us -> 228 us (1.051)
  Pallas kernels: 205 us -> 224 us
  matrix products: 3.67 us -> 0 us
    pallas_call x1, Pallas kernels: 205 us -> 224 us  [sketch_products(): pl.pallas_call(functools.partial(sketch_kernel, n_tensor, chunks), out_sh...]
    dot_general x1 -> x0, matrix products: 3.67 us -> none  [scores_of(): inner = jnp.dot(sketches, query_sketches.T, precision=lax.Precision.HIGHEST)]
    reshape x3 -> x2, local copies, waits for them, and re-layouts: 4.83 us -> 2.16 us  [fused_local(): pairs.reshape(-1, rank // 2, 2, rank).transpose(0, 2, 1, 3)]
where the time goes in v3:
time: 228 us
  Pallas kernels  224 us (98%)
  local copies, waits for them, and re-layouts  3.51 us (2%)
    pallas_call x1, Pallas kernels, sketch_products(): pl.pallas_call(functools.partial(sketch_kernel, n_tensor, chunks), out_sh...  224 us

profile of v3, /device:TPU:0, one launch (start us, length us, event | category | flops | bytes accessed | tf_op | source)
XLA Modules:
  0.0 227.8 jit_solution(5461795968909903266)
XLA Ops:
  0.6 223.6 %sketch_products.1 = (f32[512,128]{1,0:T(8,128)}, f32[16,64]{1,0:T(8,128)}) custom-call(bf16[512,1024]{1,0:T(8,128)(2,1)} %x_ref.1, bf16[256,1024]{1,0:T(8,128)(2,1)} %qx_ref.1, bf16[1024,3584]{1,0:T(8,128)(2,1)} %wg_ref.1, bf16[1024,3584]{1,0:T(8,128)(2,1)} %wu_ref.1, bf16[512,1024]{1,0:T(8,128)(2,1)} %dy_ref.1, bf16[256,1024]{1,0:T(8,128)(2,1)} %qdy_ref.1, ...), custom_call_target="tpu_custom_call" | custom-call | tf_op jit(solution)/shard_map/sketch_products/pallas_call | solution.py:468
  224.3 1.3 reshape.10
  225.5 0.1 copy.12
  225.6 0.9 reshape.11
  226.5 1.3 copy.14

commit v4 on v3

--- a/solution.py
+++ b/solution.py
@@ -92,7 +92,7 @@
     n_tensor, chunks, x_ref, qx_ref, wg_ref, wu_ref, dy_ref, qdy_ref, proj_ref, oproj_ref, ids_ref, qids_ref,
     sketch_ref, scores_ref,
     tok, wts, grads, acc, lefts, swap, parts, terms, whole,
-    halfway, spreads, grams, lqs, rqs, norms, idrows,
+    spreads, grams, lqs, rqs, norms, idrows,
     lx, lw, zs, zr, ys, yr, xs, xr, ss, sr, fs, fr, lg, ls, lr, ps, pr, ts, tr, ws, wr, qs, qr, ns, nr, ds, dr, es, er,
 ):
     group = lax.axis_index("groups")
@@ -222,12 +222,6 @@
     def work(slot, i):
         finish(slot, i, jnp.dot(tok[slot], wts[i], preferred_element_type=jnp.float32))
 
-    def side_dot(slot, i, side):
-        return jnp.dot(
-            tok[slot, :, pl.ds(pl.multiple_of(side * (2 * rows), 2 * rows), 2 * rows)],
-            wts[i, pl.ds(pl.multiple_of(side * (2 * rows), 2 * rows), 2 * rows), :],
-            preferred_element_type=jnp.float32)
-
     early = chunks // 2 + 1
     done = 0
     for h in range(1, n_tensor):
@@ -301,59 +295,60 @@
 
     spread(left[:, :train], ids_ref[...], EX_DEV, 0, train)
     spread(left[:, train:], qids_ref[...], QEX_DEV, train, left.shape[1] - train)
+    def gram(k):
+        grams[k] = lax.dot_general(
+            left[:, :train], lqs[k], (((0,), (0,)), ((), ())),
+            precision=lax.Precision.HIGHEST, preferred_element_type=jnp.float32)
+
+    gram(dp)
+
+    @pl.loop(0, n_tensor)
+    def _(shard):
+        y_copy(shard).wait_recv()
+
+    @pl.loop(0, chunks - 1)
+    def _(i):
+        work(1, i)
+
+    last = chunks - 1
+    w_copy(last, sibling, ss, sr, sibling).wait_recv()
+
+    hand_on(last)
+    w_copy(last, far, fs, fr, sibling).wait_recv()
+
+    def packed(slot):
+        return jnp.concatenate([acc[slot, :half], acc[slot, half:]], axis=1)
+
+    @pl.loop(0, 2)
+    def _(turn):
+        work(1 - turn, last)
+
+        @pl.when(turn == 0)
+        def _():
+            swap[0] = packed(1)
+            swap_copy().start()
+
     dp_copy(lqs, es, er, across, across).wait_recv()
     far_copy = pltpu.make_async_remote_copy(
         lqs.at[across], lqs.at[across], es.at[far], er.at[across],
         device_id={"dp": sibling}, device_id_type=MESH)
     far_copy.start()
-    dp_copy(lqs, es, er, sibling, sibling).wait_recv()
-    dp_copy(lqs, es, er, far, far).wait_recv()
-    for k in range(4):
-        grams[k] = lax.dot_general(
-            left[:, :train], lqs[k], (((0,), (0,)), ((), ())),
-            precision=lax.Precision.HIGHEST, preferred_element_type=jnp.float32)
-
-    @pl.loop(0, n_tensor)
-    def _(shard):
-        y_copy(shard).wait_recv()
-
-    @pl.loop(0, chunks - 1)
-    def _(i):
-        work(1, i)
-
-    last = chunks - 1
-    w_copy(last, sibling, ss, sr, sibling).wait_recv()
-
-    @pl.loop(0, 2)
-    def _(slot):
-        halfway[slot] = side_dot(slot, last, dp // 2)
-
-    hand_on(last)
-    w_copy(last, far, fs, fr, sibling).wait_recv()
-
-    def packed(slot):
-        return jnp.concatenate([acc[slot, :half], acc[slot, half:]], axis=1)
-
-    @pl.loop(0, 2)
-    def _(turn):
-        finish(1 - turn, last, halfway[1 - turn] + side_dot(1 - turn, last, 1 - dp // 2))
-
-        @pl.when(turn == 0)
-        def _():
-            swap[0] = packed(1)
-            swap_copy().start()
-
     swap_copy().wait_recv()
     parts[...] = (packed(0) + swap[1]).reshape(parts.shape)
     for to in others():
         term_copy(me, to).start()
     total = parts[me]
+    dp_copy(lqs, es, er, sibling, sibling).wait_recv()
+    gram(sibling)
+    gram(across)
     for source in others():
         term_copy(source, source).wait_recv()
         total = total + terms[source]
     whole[me] = total
     for to in others():
         whole_copy(me, to).start()
+    dp_copy(lqs, es, er, far, far).wait_recv()
+    gram(far)
     for source in others():
         whole_copy(source, source).wait_recv()
     both = whole[...].reshape(half, 2 * rank)
@@ -483,7 +478,6 @@
             pltpu.VMEM((n_tensor, tokens // 2 // n_tensor, 2 * rank), f32),
             pltpu.VMEM((n_tensor, tokens // 2 // n_tensor, 2 * rank), f32),
             pltpu.VMEM((n_tensor, tokens // 2 // n_tensor, 2 * rank), f32),
-            pltpu.VMEM((2, tokens, 2 * CHUNK), f32),
             pltpu.VMEM((2, 2, EX_DEV * rank // 2, tokens), jnp.bfloat16),
             pltpu.VMEM((4, inputs.shape[0], query_inputs.shape[0]), f32),
             pltpu.VMEM((4, rank, query_inputs.shape[0]), f32),

time: 228 us -> 208 us (0.912)
  Pallas kernels: 224 us -> 203 us
    pallas_call x1, Pallas kernels: 224 us -> 203 us  [sketch_products(): pl.pallas_call(functools.partial(sketch_kernel, n_tensor, chunks), out_sh...]
where the time goes in v4:
time: 208 us
  Pallas kernels  203 us (98%)
  local copies, waits for them, and re-layouts  3.51 us (2%)
    pallas_call x1, Pallas kernels, sketch_products(): pl.pallas_call(functools.partial(sketch_kernel, n_tensor, chunks), out_sh...  203 us

profile of v4, /device:TPU:0, one launch (start us, length us, event | category | flops | bytes accessed | tf_op | source)
XLA Modules:
  0.0 207.5 jit_solution(5815853760243587947)
XLA Ops:
  0.6 203.4 %sketch_products.1 = (f32[512,128]{1,0:T(8,128)}, f32[16,64]{1,0:T(8,128)}) custom-call(bf16[512,1024]{1,0:T(8,128)(2,1)} %x_ref.1, bf16[256,1024]{1,0:T(8,128)(2,1)} %qx_ref.1, bf16[1024,3584]{1,0:T(8,128)(2,1)} %wg_ref.1, bf16[1024,3584]{1,0:T(8,128)(2,1)} %wu_ref.1, bf16[512,1024]{1,0:T(8,128)(2,1)} %dy_ref.1, bf16[256,1024]{1,0:T(8,128)(2,1)} %qdy_ref.1, ...), custom_call_target="tpu_custom_call" | custom-call | tf_op jit(solution)/shard_map/sketch_products/pallas_call | solution.py:463
  204.0 1.3 reshape.10
  205.3 0.1 copy.12
  205.3 0.9 reshape.11
  206.2 1.3 copy.14
